TPU v7x, 32 devices: a whole 2x2x4 slice. The times are simulated.
32 devices in a mesh: rep: 2 (over x), col: 8 (over z, y), row: 2 (over core).
Axes of the slice: x: 2, y: 2, z: 4, core: 2. Of those that a mesh axis runs over, the one named last changes fastest.
Arguments:
- stored_base_codes: bfloat16 [4, 8192, 8192], P('rep', 'row', 'col'), parts along dimension 0, may hold values from -1 to 1
- previous_row_scale: float32 [4, 8192], P('rep', 'row'), parts along dimension 0, may hold values from 0.004 to 0.04
- output_side_factor: bfloat16 [4, 8192, 64], P('rep', ('row', 'col')), parts along dimension 0, may hold values from -0.75 to 0.75
- input_side_factor: bfloat16 [4, 64, 8192], P('rep', None, ('col', 'row')), parts along dimension 0, may hold values from -0.0625 to 0.0625
- magnitude: float32 [4, 8192], P('rep', 'row'), parts along dimension 0, may hold values from 8 to 32
Outputs:
- quantized: bfloat16 [4, 8192, 8192], P('rep', 'row', 'col'), parts along dimension 0
- new_scale: float32 [4, 8192], P('rep', 'row'), parts along dimension 0
There are 2 independent parts, one for each index of `rep`. A program takes and returns all parts, laid end to end along the dimension named above; each array names one. Nothing has to cross between parts.
All inputs are finite; a program needn't handle non-finite values. Where the computation divides by a largest or mean magnitude, that divisor is 1e-20 or more.
Results may differ from a plain program's by a relative error of at most 0.0044.
Values may be sent and summed in bfloat16 or wider, within the bound.
A program may use at most 192 MiB of HBM per device.

v0:
```python
import jax
import jax.numpy as jnp
from jax import lax
from jax.sharding import PartitionSpec as P

adapter_scale_factor = 0.5
epsilon = 1e-06


def merge_group(
    stored_base_codes, previous_row_scale, output_side_factor, input_side_factor, magnitude
):
    output_factor_tile = lax.all_gather(output_side_factor, "col", axis=1, tiled=True)
    input_factor_tile = lax.all_gather(input_side_factor, "row", axis=2, tiled=True)
    adapter_update_delta = jnp.einsum(
        "vfw,vwy->vfy", output_factor_tile, input_factor_tile, preferred_element_type=jnp.float32
    )
    merged_weight_rows = (
        stored_base_codes.astype(jnp.float32) * previous_row_scale[:, :, None]
        + adapter_scale_factor * adapter_update_delta
    )
    partial_sq = jnp.sum(merged_weight_rows * merged_weight_rows, axis=2)
    squares = lax.psum(partial_sq.astype(jnp.bfloat16), "col").astype(jnp.float32)
    factor = magnitude * lax.rsqrt(squares + epsilon)
    adapted = merged_weight_rows * factor[:, :, None]
    local_peak = jnp.max(jnp.abs(adapted), axis=2)
    peak_vals = lax.pmax(local_peak, "col")
    quantized = (adapted / peak_vals[:, :, None]).astype(jnp.bfloat16)
    return (quantized, peak_vals)


def per_device(
    stored_base_codes, previous_row_scale, output_side_factor, input_side_factor, magnitude
):
    quantized, new_scale = merge_group(
        stored_base_codes, previous_row_scale, output_side_factor, input_side_factor, magnitude
    )
    return (quantized, new_scale)


def solution(mesh):
    placed = (
        P("rep", "row", "col"),
        P("rep", "row"),
        P("rep", ("row", "col"), None),
        P("rep", None, ("col", "row")),
        P("rep", "row"),
    )
    return jax.shard_map(
        per_device,
        mesh=mesh,
        in_specs=placed,
        out_specs=(P("rep", "row", "col"), P("rep", "row")),
        check_vma=False,
    )
```

profile of v0, /device:TPU:0, one launch (start us, length us, event | category | flops | bytes accessed | tf_op | source)
XLA Modules:
  0.0 197.4 jit_solution(85654885651404275)
XLA Ops:
  7.2 0.0 copy-start.2
  7.2 0.0 copy-start
  7.2 0.0 all-gather.2.cloned.1.call-start
  7.2 0.7 all-gather.2.cloned.1.call-update
  7.9 21.2 %copy.7 = bf16[2,4096,1024]{1,2,0:T(8,128)(2,1)} copy(bf16[2,4096,1024]{2,1,0:T(8,128)(2,1)} %param.5) | data formatting | bytes 33554432 | tf_op args[0]
  29.2 0.0 copy-done.2
  29.2 0.0 copy-start.3
  29.2 2.2 %all_gather.7 = bf16[2,64,1024]{2,1,0:T(8,128)(2,1)S(1)} all-gather(bf16[2,64,512]{2,1,0:T(8,128)(2,1)S(1)} %copy-done.2), channel_id=1, replica_groups=mesh['rep'=2,'col'=8,'row'=2] {'row'}, dimensions={2}, use_global_device_ids=true | all-gather | bytes 393216 | tf_op jit(solution)/shard_map/all_gather | solution.py:14
  31.4 21.0 %all-gather.2.cloned.1.call-done = bf16[2,4096,64]{1,2,0:T(8,128)(2,1)} async-done(((bf16[2,512,64]{1,2,0:T(8,128)(2,1)}), bf16[2,4096,64]{1,2,0:T(8,128)(2,1)}) %all-gather.2.cloned.1.call-update) | async-done | bytes 1048592 | tf_op jit(solution)/shard_map/all_gather | solution.py:13
  52.3 0.0 copy-done
  52.3 18.4 %multiply_reduce_fusion = (bf16[2,4096]{1,0:T(2,128)(2,1)S(1)}, f32[2,4096,1024]{1,2,0:T(8,128)}) fusion(bf16[2,4096,64]{1,2,0:T(8,128)(2,1)} %all-gather.2.cloned.1.call-done, bf16[2,64,1024]{2,1,0:T(8,128)(2,1)S(1)} %all_gather.7, f32[2,4096]{1,0:T(2,128)S(1)} %copy-done, bf16[2,4096,1024]{1,2,0:T(8,128)(2,1)} %copy.7), kind=kOutput, calls=%fused_computation.2 | convolution fusion | flops 1124065280 | bytes 51691520 | tf_op jit(solution)/shard_map/vfw,vwy->vfy/dot_general | solution.py:15
  70.7 35.1 %psum.7 = bf16[2,4096]{1,0:T(2,128)(2,1)S(1)} all-reduce(bf16[2,4096]{1,0:T(2,128)(2,1)S(1)} %get-tuple-element.4), channel_id=1, replica_groups=mesh['rep'=2,'col'=8,'row'=2] {'col'}, use_global_device_ids=true, to_apply=%region_1.0 | all-reduce | flops 8192 | bytes 32768 | tf_op jit(solution)/shard_map/psum | solution.py:23
  105.7 0.0 copy-done.3
  105.8 12.0 %abs_reduce_fusion = f32[2,4096]{1,0:T(2,128)S(1)} fusion(f32[2,4096,1024]{1,2,0:T(8,128)} %get-tuple-element.5, f32[2,4096]{1,0:T(2,128)S(1)} %rsqrt_multiply_fusion), kind=kLoop, calls=%fused_computation.1 | loop fusion | flops 25157632 | bytes 33619968 | tf_op jit(solution)/shard_map/reduce_max | solution.py:26
  117.8 33.1 %pmax.7 = f32[2,4096]{1,0:T(2,128)S(1)} all-reduce(f32[2,4096]{1,0:T(2,128)S(1)} %abs_reduce_fusion), channel_id=1, replica_groups=mesh['rep'=2,'col'=8,'row'=2] {'col'}, use_global_device_ids=true, to_apply=%region_3.0 | all-reduce | flops 8192 | bytes 65536 | tf_op jit(solution)/shard_map/pmax | solution.py:27
  150.8 0.0 copy-start.1
  150.8 18.5 %divide_convert_fusion = bf16[2,4096,1024]{1,2,0:T(8,128)(2,1)} fusion(f32[2,4096,1024]{1,2,0:T(8,128)} %get-tuple-element.5, f32[2,4096]{1,0:T(2,128)S(1)} %pmax.7, f32[2,4096]{1,0:T(2,128)S(1)} %rsqrt_multiply_fusion), kind=kLoop, calls=%fused_computation | loop fusion | flops 25165824 | bytes 50397184 | tf_op jit(solution)/shard_map/convert_element_type | solution.py:28
  169.3 21.2 %copy.8 = bf16[2,4096,1024]{2,1,0:T(8,128)(2,1)} copy(bf16[2,4096,1024]{1,2,0:T(8,128)(2,1)} %divide_convert_fusion) | data formatting | bytes 33554432
  190.5 0.0 copy-done.1
  (1 shorter events, 0.0 us)
Async XLA Ops:
  7.2 22.0 %copy-start.2 = (bf16[2,64,512]{2,1,0:T(8,128)(2,1)S(1)}, bf16[2,64,512]{2,1,0:T(8,128)(2,1)}, u32[]{:S(2)}) copy-start(bf16[2,64,512]{2,1,0:T(8,128)(2,1)} %param.8) | copy-start | bytes 393220
  7.2 45.2 %copy-start = (f32[2,4096]{1,0:T(2,128)S(1)}, f32[2,4096]{1,0:T(2,128)}, u32[]{:S(2)}) copy-start(f32[2,4096]{1,0:T(2,128)} %param.6) | copy-start | bytes 98308
  7.2 45.1 %all-gather.2.cloned.1.call-start = ((), (), s32[]{:S(2)}) async-start(), calls=%async_computation | async-start | bytes 1179648 | tf_op jit(solution)/shard_map/all_gather | solution.py:13
  29.2 76.6 %copy-start.3 = (f32[2,4096]{1,0:T(2,128)S(1)}, f32[2,4096]{1,0:T(2,128)}, u32[]{:S(2)}) copy-start(f32[2,4096]{1,0:T(2,128)} %param.9) | copy-start | bytes 98308
  150.8 39.7 %copy-start.1 = (f32[2,4096]{1,0:T(2,128)}, f32[2,4096]{1,0:T(2,128)S(1)}, u32[]{:S(2)}) copy-start(f32[2,4096]{1,0:T(2,128)S(1)} %pmax.7) | copy-start | bytes 98308
Sparse Core Ops, SparseCore 0:
  10.1 42.2 all-gather.1
where the time goes:
time: 199 us; the launch traced here: 197 us
  blocking collectives  70.3 us (35%)
  local copies, waits for them, and re-layouts  42.4 us (21%)
  other arithmetic  30.5 us (15%)
  waiting for transfers between devices  21.6 us (11%)
  matrix products  18.4 us (9%)
  between operations  14.1 us (7%)
    unnamed x10, local copies, waits for them, and re-layouts  42.4 us
    psum x1, blocking collectives, merge_group(): lax.psum(partial_sq.astype(jnp.bfloat16), 'col').astype(jnp.float32)  35.1 us
    pmax x1, blocking collectives, merge_group(): peak_vals = lax.pmax(local_peak, 'col')  33.1 us
    all_gather x1, waiting for transfers between devices, merge_group(): lax.all_gather(output_side_factor, 'col', axis=1, tiled=True)  21 us
    convert_element_type x1, other arithmetic, merge_group(): quantized = (adapted / peak_vals[:, :, None]).astype(jnp.bfloat16)  18.5 us
    dot_general x1, matrix products, merge_group(): jnp.einsum('vfw,vwy->vfy', output_factor_tile, input_factor_tile, preferr...  18.4 us
    reduce_max x1, other arithmetic, merge_group(): local_peak = jnp.max(jnp.abs(adapted), axis=2)  12 us
  transfers between devices with their start and end apart: 1, of which 1 were waited for; matrix products, arithmetic and copies ran while one was open for 11% of the time, Pallas kernels for 0%

commit v1 on v0

v1 whole, which is shorter than its diff:
```python
import functools
import jax
import jax.numpy as jnp
from jax import lax
from jax.experimental import pallas as pl
from jax.experimental.pallas import tpu as pltpu
from jax.sharding import PartitionSpec as P

LANES = 128
epsilon = 1e-06
MESH = pl.DeviceIdType.MESH
resident = pltpu.VMEM
pin = pltpu.with_memory_space_constraint


def xor(a, b, size):
    total, bit = 0, 1
    while bit < size:
        total = total + ((a // bit + b // bit) % 2) * bit
        bit *= 2
    return total


def column(row):
    return jnp.transpose(jnp.broadcast_to(row, (LANES, LANES)))


def merge_kernel(
    dims, codes, prev, a, b, mag, merged, res,
    a_all, b_all, b_pad, part, parts_in, res_scr,
    code_sem, b_sem, z_send, y_send, a_recv, st_send, st_recv, bc_send, bc_recv,
):
    n, nz, ny, rows, cr, width, rank = dims
    chunks = rows // cr
    subs = cr // LANES
    kinds = 2 * subs
    me = lax.axis_index("col")
    core = lax.axis_index("row")
    z, y = me // ny, me % ny

    def source(t):
        k, q, j = t // (chunks * ny), (t // ny) % chunks, t % ny
        src = xor(z, k, nz) * ny + (y + j) % ny
        return k, q, j, src

    def code_copy(t):
        _, q, _, src = source(t)
        at = pl.ds(pl.multiple_of(src * rows + q * cr, cr), cr)
        return pltpu.make_async_copy(codes.at[:, at], merged.at[:, at], code_sem.at[t])

    tiles = n * chunks

    @pl.loop(0, tiles)
    def _(t):
        code_copy(t).start()

    barrier = pltpu.get_barrier_semaphore()
    pl.semaphore_signal(barrier, inc=1, device_id={"row": 1 - core}, device_id_type=MESH)

    @pl.loop(1, n)
    def _(t):
        pl.semaphore_signal(
            barrier, inc=1, device_id={"col": (me + t) % n}, device_id_type=MESH
        )

    packed = jnp.transpose(
        a[...].astype(jnp.float32).reshape(2 * rank, rows)
    ).astype(jnp.bfloat16)
    for q in range(chunks):
        a_all[q, me] = packed[q * cr:(q + 1) * cr]
    b_all[core] = b[...]
    pl.semaphore_wait(barrier, n)

    b_copy = pltpu.make_async_remote_copy(
        b, b_all.at[core], b_sem.at[0], b_sem.at[1],
        device_id={"row": 1 - core}, device_id_type=MESH,
    )
    b_copy.start()

    def z_copy(q, k):
        return pltpu.make_async_remote_copy(
            a_all.at[q, me], a_all.at[q, me], z_send.at[q, k], a_recv.at[q, me],
            device_id={"col": xor(z, k, nz) * ny + y}, device_id_type=MESH,
        )

    def y_copy(q, k):
        src = xor(z, k, nz) * ny + y
        return pltpu.make_async_remote_copy(
            a_all.at[q, src], a_all.at[q, src], y_send.at[q, k], a_recv.at[q, src],
            device_id={"col": z * ny + (y + 1) % ny}, device_id_type=MESH,
        )

    if ny > 1:
        for q in range(chunks):
            y_copy(q, 0).start()

    @pl.loop(1, nz)
    def _(k):
        for q in range(chunks):
            z_copy(q, k).start()

    b_copy.wait_recv()
    b_pad[...] = jnp.zeros_like(b_pad)
    cols = b.shape[2]
    for p in range(2):
        for r in range(2):
            b_pad[p, p * rank:(p + 1) * rank, r * cols:(r + 1) * cols] = b_all[r, p]

    def part_copy(q, src):
        return pltpu.make_async_remote_copy(
            part.at[q, src], parts_in.at[q, me], st_send.at[q, src], st_recv.at[q, me],
            device_id={"col": src}, device_id_type=MESH,
        )

    def arrived(ref, sem):
        pltpu.make_async_copy(ref, ref, sem).wait()

    block = 256 if width % 256 == 0 else LANES

    @pl.loop(0, tiles)
    def _(t):
        k, q, j, src = source(t)

        @pl.when(src != me)
        def _():
            arrived(a_all.at[q, src], a_recv.at[q, src])

        if ny > 1:
            @pl.when((j == 0) & (k > 0))
            def _():
                y_copy(q, k).start()

        code_copy(t).wait()
        for p in range(2):
            for s in range(subs):
                base = pl.multiple_of(src * rows + q * cr + s * LANES, LANES)
                at = pl.ds(base, LANES)
                scale = column(2.0 * prev[p:p + 1, at])
                lhs = a_all[q, src, s * LANES:(s + 1) * LANES]
                squares = jnp.zeros((LANES, LANES), jnp.float32)
                peaks = jnp.zeros((LANES, LANES), jnp.float32)
                for c in range(0, width, block):
                    delta = jnp.dot(
                        lhs, b_pad[p, :, c:c + block], preferred_element_type=jnp.float32
                    )
                    for d in range(0, block, LANES):
                        here = slice(c + d, c + d + LANES)
                        m = (
                            merged[p, at, here].astype(jnp.float32) * scale
                            + delta[:, d:d + LANES]
                        )
                        merged[p, at, here] = m.astype(jnp.bfloat16)
                        squares += m * m
                        peaks = jnp.maximum(peaks, jnp.abs(m))
                i = p * subs + s
                part[q, src, i:i + 1] = jnp.sum(squares.T, axis=0, keepdims=True)
                part[q, src, kinds + i:kinds + i + 1] = jnp.max(
                    peaks.T, axis=0, keepdims=True
                )

        @pl.when(src != me)
        def _():
            part_copy(q, src).start()

        @pl.when(src == me)
        def _():
            parts_in[q, me] = part[q, me]

    def res_copy(q, c):
        return pltpu.make_async_remote_copy(
            res_scr.at[q, me], res_scr.at[q, me], bc_send.at[q, c], bc_recv.at[q, me],
            device_id={"col": c}, device_id_type=MESH,
        )

    for q in range(chunks):
        @pl.loop(1, n)
        def _(t):
            c = (me + t) % n
            arrived(parts_in.at[q, c], st_recv.at[q, c])

        got = parts_in[q]
        squares = jnp.sum(got[:, :kinds], axis=0)
        peaks = jnp.max(got[:, kinds:], axis=0)
        for p in range(2):
            for s in range(subs):
                i = p * subs + s
                at = pl.ds(pl.multiple_of(me * rows + q * cr + s * LANES, LANES), LANES)
                factor = mag[p:p + 1, at] * lax.rsqrt(0.25 * squares[i:i + 1] + epsilon)
                peak = peaks[i:i + 1]
                res_scr[q, me, i:i + 1] = peak
                res_scr[q, me, kinds + i:kinds + i + 1] = 0.5 * peak * factor

        @pl.loop(1, n)
        def _(t):
            res_copy(q, (me + t) % n).start()

    b_copy.wait_send()
    for q in range(chunks):
        @pl.loop(1, nz)
        def _(k):
            z_copy(q, k).wait_send()

        if ny > 1:
            @pl.loop(0, nz)
            def _(k):
                y_copy(q, k).wait_send()

        @pl.loop(1, n)
        def _(t):
            c = (me + t) % n
            part_copy(q, c).wait_send()
            res_copy(q, c).wait_send()
            arrived(res_scr.at[q, c], bc_recv.at[q, c])

    res[...] = res_scr[...]


def scale_kernel(dims, slots, merged, res, out, new_scale, held, sem):
    n, nz, ny, rows, cr, width, rank = dims
    chunks = rows // cr
    subs = cr // LANES
    kinds = 2 * subs
    tiles = n * chunks

    def out_copy(t, slot):
        at = pl.ds(pl.multiple_of(t * cr, cr), cr)
        return pltpu.make_async_copy(held.at[slot], out.at[:, at], sem.at[slot])

    @pl.loop(0, tiles)
    def _(t):
        slot = t % slots
        src, q = t // chunks, t % chunks

        @pl.when(t >= slots)
        def _():
            out_copy(t - slots, slot).wait()

        for p in range(2):
            for s in range(subs):
                i = p * subs + s
                at = pl.ds(pl.multiple_of(t * cr + s * LANES, LANES), LANES)
                inverse = column(1.0 / res[q, src, i:i + 1])
                new_scale[p:p + 1, at] = res[q, src, kinds + i:kinds + i + 1]
                for c in range(0, width, LANES):
                    held[slot, p, s * LANES:(s + 1) * LANES, c:c + LANES] = (
                        merged[p, at, c:c + LANES].astype(jnp.float32) * inverse
                    ).astype(jnp.bfloat16)
        out_copy(t, slot).start()

    @pl.loop(tiles - min(slots, tiles), tiles)
    def _(t):
        out_copy(t, t % slots).wait()


def per_device(n, codes, prev, a, b, mag):
    _, out_rows, width = codes.shape
    _, rows, rank = a.shape
    cr = min(rows, 256)
    ny = 2 if n == 8 else 1
    nz = n // ny
    chunks = rows // cr
    stat = 4 * (cr // LANES)
    dims = (n, nz, ny, rows, cr, width, rank)
    vmem = pl.BlockSpec(memory_space=pltpu.VMEM)
    dma = pltpu.SemaphoreType.DMA
    merged, res = pl.pallas_call(
        functools.partial(merge_kernel, dims),
        out_shape=(
            resident(codes.shape, jnp.bfloat16),
            resident((chunks, n, stat, LANES), jnp.float32),
        ),
        in_specs=[pl.BlockSpec(memory_space=pltpu.HBM), vmem, vmem, vmem, vmem],
        out_specs=(vmem, vmem),
        scratch_shapes=[
            pltpu.VMEM((chunks, n, cr, 2 * rank), jnp.bfloat16),
            pltpu.VMEM((2,) + b.shape, jnp.bfloat16),
            pltpu.VMEM((2, 2 * rank, width), jnp.bfloat16),
            pltpu.VMEM((chunks, n, stat, LANES), jnp.float32),
            pltpu.VMEM((chunks, n, stat, LANES), jnp.float32),
            pltpu.VMEM((chunks, n, stat, LANES), jnp.float32),
            dma((n * chunks,)),
            dma((2,)),
            dma((chunks, nz)),
            dma((chunks, nz)),
            dma((chunks, n)),
            dma((chunks, n)),
            dma((chunks, n)),
            dma((chunks, n)),
            dma((chunks, n)),
        ],
        compiler_params=pltpu.CompilerParams(
            collective_id=0, has_side_effects=True, vmem_limit_bytes=16 * 2**20
        ),
        name="merge",
    )(pin(codes, pltpu.HBM), prev, jnp.swapaxes(a, 1, 2), b, mag)
    slots = 4
    return pl.pallas_call(
        functools.partial(scale_kernel, dims, slots),
        out_shape=(
            jax.ShapeDtypeStruct(codes.shape, jnp.bfloat16),
            jax.ShapeDtypeStruct(prev.shape, jnp.float32),
        ),
        in_specs=[vmem, vmem],
        out_specs=(pl.BlockSpec(memory_space=pl.ANY), vmem),
        scratch_shapes=[
            pltpu.VMEM((slots, 2, cr, width), jnp.bfloat16),
            dma((slots,)),
        ],
        compiler_params=pltpu.CompilerParams(vmem_limit_bytes=16 * 2**20),
        name="rescale",
    )(
        pin(merged, pltpu.VMEM),
        pin(res, pltpu.VMEM),
    )


def solution(mesh):
    placed = (
        P("rep", "row", "col"),
        P("rep", "row"),
        P("rep", ("row", "col"), None),
        P("rep", None, ("col", "row")),
        P("rep", "row"),
    )
    return jax.shard_map(
        functools.partial(per_device, mesh.shape["col"]),
        mesh=mesh,
        in_specs=placed,
        out_specs=(P("rep", "row", "col"), P("rep", "row")),
        check_vma=False,
    )
```

time: 199 us -> 57.4 us (0.29)
  blocking collectives: 70.3 us -> 0 us
  Pallas kernels: 0 us -> 53.1 us
  local copies, waits for them, and re-layouts: 42.4 us -> 3.32 us
  other arithmetic: 30.5 us -> 0 us
  waiting for transfers between devices: 21.6 us -> 0 us
  matrix products: 18.4 us -> 0 us
  between operations: 14.1 us -> 0.65 us
    pallas_call x0 -> x2, Pallas kernels: none -> 53.1 us  [the longest x1 46.4 us: per_device(): pl.pallas_call(functools.partial(merge_kernel, dims), out_shape=(resident...]
    unnamed x10 -> x8, local copies, waits for them, and re-layouts: 42.4 us -> 3.32 us
    psum x1 -> x0, blocking collectives: 35.1 us -> none  [merge_group(): lax.psum(partial_sq.astype(jnp.bfloat16), 'col').astype(jnp.float32)]
    pmax x1 -> x0, blocking collectives: 33.1 us -> none  [merge_group(): peak_vals = lax.pmax(local_peak, 'col')]
    all_gather x1 -> x0, waiting for transfers between devices: 21 us -> none  [merge_group(): lax.all_gather(output_side_factor, 'col', axis=1, tiled=True)]
    convert_element_type x1 -> x0, other arithmetic: 18.5 us -> none  [merge_group(): quantized = (adapted / peak_vals[:, :, None]).astype(jnp.bfloat16)]
    dot_general x1 -> x0, matrix products: 18.4 us -> none  [merge_group(): jnp.einsum('vfw,vwy->vfy', output_factor_tile, input_factor_tile, preferr...]
    reduce_max x1 -> x0, other arithmetic: 12 us -> none  [merge_group(): local_peak = jnp.max(jnp.abs(adapted), axis=2)]
  transfers between devices with their start and end apart: 1 -> 0, of which waited for: 1 -> 0; matrix products, arithmetic and copies ran while one was open for 11% -> 0% of each run, Pallas kernels for 0% -> 0%
where the time goes in v1:
time: 57.4 us; the launch traced here: 57.1 us
  Pallas kernels  53.1 us (93%)
  local copies, waits for them, and re-layouts  3.32 us (6%)
  between operations  0.65 us (1%)
    pallas_call x1, Pallas kernels, per_device(): pl.pallas_call(functools.partial(merge_kernel, dims), out_shape=(resident...  46.4 us
    pallas_call x1, Pallas kernels, per_device(): pl.pallas_call(functools.partial(scale_kernel, dims, slots), out_shape=(j...  6.76 us
    unnamed x8, local copies, waits for them, and re-layouts  3.32 us

profile of v1, /device:TPU:0, one launch (start us, length us, event | category | flops | bytes accessed | tf_op | source)
XLA Modules:
  0.0 57.1 jit_solution(17734624526455645846)
XLA Ops:
  0.6 0.0 copy-start
  0.6 0.9 %copy-done = bf16[2,512,64]{1,2,0:T(8,128)(2,1)S(1)} copy-done((bf16[2,512,64]{1,2,0:T(8,128)(2,1)S(1)}, bf16[2,512,64]{1,2,0:T(8,128)(2,1)}, u32[]{:S(2)}) %copy-start) | copy-done | bytes 131096
  1.5 0.0 copy-start.1
  1.5 0.9 %copy-done.1 = bf16[2,64,512]{2,1,0:T(8,128)(2,1)S(1)} copy-done((bf16[2,64,512]{2,1,0:T(8,128)(2,1)S(1)}, bf16[2,64,512]{2,1,0:T(8,128)(2,1)}, u32[]{:S(2)}) %copy-start.1) | copy-done | bytes 131096
  2.4 0.0 copy-start.2
  2.4 0.8 %copy-done.2 = f32[2,4096]{1,0:T(2,128)S(1)} copy-done((f32[2,4096]{1,0:T(2,128)S(1)}, f32[2,4096]{1,0:T(2,128)}, u32[]{:S(2)}) %copy-start.2) | copy-done | bytes 32792
  3.2 0.0 copy-start.3
  3.2 0.8 %copy-done.3 = f32[2,4096]{1,0:T(2,128)S(1)} copy-done((f32[2,4096]{1,0:T(2,128)S(1)}, f32[2,4096]{1,0:T(2,128)}, u32[]{:S(2)}) %copy-start.3) | copy-done | bytes 32792
  4.0 46.4 %merge.1 = (bf16[2,4096,1024]{2,1,0:T(8,128)(2,1)S(1)}, f32[2,8,8,128]{3,2,1,0:T(8,128)S(1)}) custom-call(bf16[2,4096,1024]{2,1,0:T(8,128)(2,1)} %codes.1, f32[2,4096]{1,0:T(2,128)S(1)} %copy-done.2, bf16[2,64,512]{2,1,0:T(8,128)(2,1)S(1)} %bitcast.1, bf16[2,64,512]{2,1,0:T(8,128)(2,1)S(1)} %copy-done.1, f32[2,4096]{1,0:T(2,128)S(1)} %copy-done.3), custom_call_target="tpu_custom_call" | custom-call | tf_op jit(solution)/shard_map/merge/pallas_call | solution.py:266
  50.4 6.8 %rescale.1 = (bf16[2,4096,1024]{2,1,0:T(8,128)(2,1)}, f32[2,4096]{1,0:T(2,128)}) custom-call(bf16[2,4096,1024]{2,1,0:T(8,128)(2,1)S(1)} %get-tuple-element.4.merged, f32[2,8,8,128]{3,2,1,0:T(8,128)S(1)} %get-tuple-element.5.res), custom_call_target="tpu_custom_call" | custom-call | tf_op jit(solution)/shard_map/rescale/pallas_call | solution.py:297
Async XLA Ops:
  0.6 0.9 %copy-start = (bf16[2,512,64]{1,2,0:T(8,128)(2,1)S(1)}, bf16[2,512,64]{1,2,0:T(8,128)(2,1)}, u32[]{:S(2)}) copy-start(bf16[2,512,64]{1,2,0:T(8,128)(2,1)} %param.7) | copy-start | bytes 393220
  1.5 0.9 %copy-start.1 = (bf16[2,64,512]{2,1,0:T(8,128)(2,1)S(1)}, bf16[2,64,512]{2,1,0:T(8,128)(2,1)}, u32[]{:S(2)}) copy-start(bf16[2,64,512]{2,1,0:T(8,128)(2,1)} %b.1) | copy-start | bytes 393220
  2.4 0.8 %copy-start.2 = (f32[2,4096]{1,0:T(2,128)S(1)}, f32[2,4096]{1,0:T(2,128)}, u32[]{:S(2)}) copy-start(f32[2,4096]{1,0:T(2,128)} %prev.1) | copy-start | bytes 98308
  3.2 0.8 %copy-start.3 = (f32[2,4096]{1,0:T(2,128)S(1)}, f32[2,4096]{1,0:T(2,128)}, u32[]{:S(2)}) copy-start(f32[2,4096]{1,0:T(2,128)} %mag.1) | copy-start | bytes 98308

commit v2 on v1

v2 whole, which is shorter than its diff:
```python
import functools
import jax
import jax.numpy as jnp
from jax import lax
from jax.experimental import pallas as pl
from jax.experimental.pallas import tpu as pltpu
from jax.sharding import PartitionSpec as P

LANES = 128
epsilon = 1e-06
MESH = pl.DeviceIdType.MESH
resident = pltpu.VMEM
pin = pltpu.with_memory_space_constraint


def column(row):
    return jnp.transpose(jnp.broadcast_to(row, (LANES, LANES)))


def merge_kernel(
    dims, codes, prev_hbm, a_hbm, b_hbm, mag_hbm, merged, res,
    prev, a, b, mag, a_all, b_all, b_pad, part, parts_in, res_scr,
    in_sem, code_sem, b_sem, z_send, y_send, a_recv, st_send, st_recv, bc_send, bc_recv,
):
    n, nz, ny, rows, cr, width, rank = dims
    chunks = rows // cr
    subs = cr // LANES
    kinds = 2 * subs
    me = lax.axis_index("col")
    core = lax.axis_index("row")
    z, y = me // ny, me % ny
    beside = z * ny + (y + 1) % ny
    split = chunks - chunks // 2

    small = [
        pltpu.make_async_copy(src, dst, in_sem.at[i])
        for i, (src, dst) in enumerate(
            [(a_hbm, a), (b_hbm, b), (prev_hbm, prev), (mag_hbm, mag)]
        )
    ]
    for copy in small:
        copy.start()

    barrier = pltpu.get_barrier_semaphore()
    pl.semaphore_signal(barrier, inc=1, device_id={"row": 1 - core}, device_id_type=MESH)

    @pl.loop(1, n)
    def _(t):
        pl.semaphore_signal(
            barrier, inc=1, device_id={"col": (me + t) % n}, device_id_type=MESH
        )

    def at_place(e):
        far, down = (e + 1) // 2, (e + 1) % 2
        zs = jnp.where(down == 1, z - far, z + far)
        return far, down, zs, (zs >= 0) & (zs < nz)

    def code_copy(q, src):
        at = pl.ds(pl.multiple_of(src * rows + q * cr, cr), cr)
        return pltpu.make_async_copy(
            codes.at[:, at], merged.at[:, at], code_sem.at[q, src]
        )

    steps = (2 * nz - 1) * chunks * ny

    def place(t):
        first = ny * chunks
        late = t >= first
        u = jnp.where(late, t - first, 0)
        ring = (2 * nz - 2) * chunks
        e = jnp.where(late, 1 + (u % ring) // chunks, 0)
        j = jnp.where(late, u // ring, t // chunks)
        return e, t % chunks, j

    @pl.loop(0, steps)
    def _(t):
        e, q, j = place(t)
        _, _, zs, valid = at_place(e)

        @pl.when(valid)
        def _():
            code_copy(q, zs * ny + (y + j) % ny).start()

    small[0].wait()
    packed = jnp.transpose(
        a[...].astype(jnp.float32).reshape(2 * rank, rows)
    ).astype(jnp.bfloat16)
    for q in range(chunks):
        a_all[q, me] = packed[q * cr:(q + 1) * cr]
    small[1].wait()
    b_all[core] = b[...]
    pl.semaphore_wait(barrier, n)

    def a_copy(q, src, to, sem):
        return pltpu.make_async_remote_copy(
            a_all.at[q, src], a_all.at[q, src], sem, a_recv.at[q, src],
            device_id={"col": to}, device_id_type=MESH,
        )

    def up_copy(q, src):
        return a_copy(q, src, me + ny, z_send.at[0, q, src])

    def down_copy(q, src):
        return a_copy(q, src, me - ny, z_send.at[1, q, src])

    def y_copy(q, src):
        return a_copy(q, src, beside, y_send.at[q, src])

    b_copy = pltpu.make_async_remote_copy(
        b, b_all.at[core], b_sem.at[0], b_sem.at[1],
        device_id={"row": 1 - core}, device_id_type=MESH,
    )
    b_copy.start()

    def pass_on(e, q, j, action):
        far, down, zs, _ = at_place(e)
        src = zs * ny + (y + j) % ny
        along = (j == 0) | ((e == 0) & (q >= split))
        up = along & (z + 1 < nz) & ((e == 0) | (down == 1))
        below = along & (z > 0) & ((e == 0) | (down == 0))

        if ny > 1:
            @pl.when((j == 0) & ((far != 1) | (q < split)))
            def _():
                action(y_copy(q, src))

        @pl.when(up)
        def _():
            action(up_copy(q, src))

        @pl.when(below)
        def _():
            action(down_copy(q, src))

    for q in range(chunks):
        pass_on(0, q, 0, lambda copy: copy.start())

    small[2].wait()
    small[3].wait()
    b_copy.wait_recv()
    cols = b.shape[2]
    b_pad[...] = jnp.zeros_like(b_pad)
    for p in range(2):
        for r in range(2):
            b_pad[p, p * rank:(p + 1) * rank, r * cols:(r + 1) * cols] = b_all[r, p]

    def part_copy(src):
        return pltpu.make_async_remote_copy(
            part.at[src], parts_in.at[me], st_send.at[src], st_recv.at[me],
            device_id={"col": src}, device_id_type=MESH,
        )

    def arrived(ref, sem):
        pltpu.make_async_copy(ref, ref, sem).wait()

    block = 256 if width % 256 == 0 else LANES

    def tile(q, src):
        code_copy(q, src).wait()
        for p in range(2):
            for s in range(subs):
                base = pl.multiple_of(src * rows + q * cr + s * LANES, LANES)
                at = pl.ds(base, LANES)
                scale = column(2.0 * prev[p:p + 1, at])
                lhs = a_all[q, src, s * LANES:(s + 1) * LANES]
                squares = jnp.zeros((LANES, LANES), jnp.float32)
                peaks = jnp.zeros((LANES, LANES), jnp.float32)
                for c in range(0, width, block):
                    delta = jnp.dot(
                        lhs, b_pad[p, :, c:c + block], preferred_element_type=jnp.float32
                    )
                    for d in range(0, block, LANES):
                        here = slice(c + d, c + d + LANES)
                        m = (
                            merged[p, at, here].astype(jnp.float32) * scale
                            + delta[:, d:d + LANES]
                        )
                        merged[p, at, here] = m.astype(jnp.bfloat16)
                        squares += m * m
                        peaks = jnp.maximum(peaks, jnp.abs(m))
                i = p * subs + s
                part[src, q, i:i + 1] = jnp.sum(squares.T, axis=0, keepdims=True)
                part[src, q, kinds + i:kinds + i + 1] = jnp.max(
                    peaks.T, axis=0, keepdims=True
                )

    @pl.loop(0, steps)
    def _(t):
        e, q, j = place(t)
        _, _, zs, valid = at_place(e)
        src = zs * ny + (y + j) % ny

        @pl.when(valid)
        def _():
            @pl.when((e != 0) | (j != 0))
            def _():
                arrived(a_all.at[q, src], a_recv.at[q, src])
                pass_on(e, q, j, lambda copy: copy.start())

            tile(q, src)

            @pl.when(((e != 0) | (j != 0)) & (q == chunks - 1))
            def _():
                part_copy(src).start()

            @pl.when((e == 0) & (j == 0))
            def _():
                parts_in[src, q] = part[src, q]

    def res_copy(c):
        return pltpu.make_async_remote_copy(
            res_scr.at[me], res_scr.at[me], bc_send.at[c], bc_recv.at[me],
            device_id={"col": c}, device_id_type=MESH,
        )

    @pl.loop(1, n)
    def _(t):
        c = (me + t) % n
        arrived(parts_in.at[c], st_recv.at[c])

    for q in range(chunks):
        got = parts_in[:, q]
        squares = jnp.sum(got[:, :kinds], axis=0)
        peaks = jnp.max(got[:, kinds:], axis=0)
        for p in range(2):
            for s in range(subs):
                i = p * subs + s
                at = pl.ds(pl.multiple_of(me * rows + q * cr + s * LANES, LANES), LANES)
                factor = mag[p:p + 1, at] * lax.rsqrt(0.25 * squares[i:i + 1] + epsilon)
                peak = peaks[i:i + 1]
                res_scr[me, q, i:i + 1] = peak
                res_scr[me, q, kinds + i:kinds + i + 1] = 0.5 * peak * factor

    @pl.loop(1, n)
    def _(t):
        res_copy((me + t) % n).start()

    b_copy.wait_send()

    @pl.loop(0, steps)
    def _(t):
        e, q, j = place(t)
        _, _, _, valid = at_place(e)

        @pl.when(valid)
        def _():
            pass_on(e, q, j, lambda copy: copy.wait_send())

    @pl.loop(1, n)
    def _(t):
        c = (me + t) % n
        part_copy(c).wait_send()
        res_copy(c).wait_send()
        arrived(res_scr.at[c], bc_recv.at[c])

    res[...] = res_scr[...]


def scale_kernel(dims, slots, merged, res, out, new_scale, held, sem):
    n, nz, ny, rows, cr, width, rank = dims
    chunks = rows // cr
    subs = cr // LANES
    kinds = 2 * subs
    tiles = n * chunks

    def out_copy(t, slot):
        at = pl.ds(pl.multiple_of(t * cr, cr), cr)
        return pltpu.make_async_copy(held.at[slot], out.at[:, at], sem.at[slot])

    @pl.loop(0, tiles)
    def _(t):
        slot = t % slots
        src, q = t // chunks, t % chunks

        @pl.when(t >= slots)
        def _():
            out_copy(t - slots, slot).wait()

        for p in range(2):
            for s in range(subs):
                i = p * subs + s
                at = pl.ds(pl.multiple_of(t * cr + s * LANES, LANES), LANES)
                inverse = column(1.0 / res[src, q, i:i + 1])
                new_scale[p:p + 1, at] = res[src, q, kinds + i:kinds + i + 1]
                for c in range(0, width, LANES):
                    held[slot, p, s * LANES:(s + 1) * LANES, c:c + LANES] = (
                        merged[p, at, c:c + LANES].astype(jnp.float32) * inverse
                    ).astype(jnp.bfloat16)
        out_copy(t, slot).start()

    @pl.loop(tiles - min(slots, tiles), tiles)
    def _(t):
        out_copy(t, t % slots).wait()


def per_device(n, codes, prev, a, b, mag):
    _, out_rows, width = codes.shape
    _, rows, rank = a.shape
    cr = min(rows, 256)
    ny = 2 if n == 8 else 1
    nz = n // ny
    chunks = rows // cr
    stat = 4 * (cr // LANES)
    dims = (n, nz, ny, rows, cr, width, rank)
    vmem = pl.BlockSpec(memory_space=pltpu.VMEM)
    hbm = pl.BlockSpec(memory_space=pltpu.HBM)
    a = jnp.swapaxes(a, 1, 2)
    dma = pltpu.SemaphoreType.DMA
    merged, res = pl.pallas_call(
        functools.partial(merge_kernel, dims),
        out_shape=(
            resident(codes.shape, jnp.bfloat16),
            resident((n, chunks, stat, LANES), jnp.float32),
        ),
        in_specs=[hbm] * 5,
        out_specs=(vmem, vmem),
        scratch_shapes=[
            pltpu.VMEM(prev.shape, jnp.float32),
            pltpu.VMEM(a.shape, jnp.bfloat16),
            pltpu.VMEM(b.shape, jnp.bfloat16),
            pltpu.VMEM(mag.shape, jnp.float32),
            pltpu.VMEM((chunks, n, cr, 2 * rank), jnp.bfloat16),
            pltpu.VMEM((2,) + b.shape, jnp.bfloat16),
            pltpu.VMEM((2, 2 * rank, width), jnp.bfloat16),
            pltpu.VMEM((n, chunks, stat, LANES), jnp.float32),
            pltpu.VMEM((n, chunks, stat, LANES), jnp.float32),
            pltpu.VMEM((n, chunks, stat, LANES), jnp.float32),
            dma((4,)),
            dma((chunks, n)),
            dma((2,)),
            dma((2, chunks, n)),
            dma((chunks, n)),
            dma((chunks, n)),
            dma((n,)),
            dma((n,)),
            dma((n,)),
            dma((n,)),
        ],
        compiler_params=pltpu.CompilerParams(
            collective_id=0, has_side_effects=True, vmem_limit_bytes=16 * 2**20
        ),
        name="merge",
    )(*(pin(x, pltpu.HBM) for x in (codes, prev, a, b, mag)))
    slots = 4
    return pl.pallas_call(
        functools.partial(scale_kernel, dims, slots),
        out_shape=(
            jax.ShapeDtypeStruct(codes.shape, jnp.bfloat16),
            jax.ShapeDtypeStruct(prev.shape, jnp.float32),
        ),
        in_specs=[vmem, vmem],
        out_specs=(pl.BlockSpec(memory_space=pl.ANY), vmem),
        scratch_shapes=[
            pltpu.VMEM((slots, 2, cr, width), jnp.bfloat16),
            dma((slots,)),
        ],
        compiler_params=pltpu.CompilerParams(vmem_limit_bytes=16 * 2**20),
        name="rescale",
    )(
        pin(merged, pltpu.VMEM),
        pin(res, pltpu.VMEM),
    )


def solution(mesh):
    placed = (
        P("rep", "row", "col"),
        P("rep", "row"),
        P("rep", ("row", "col"), None),
        P("rep", None, ("col", "row")),
        P("rep", "row"),
    )
    return jax.shard_map(
        functools.partial(per_device, mesh.shape["col"]),
        mesh=mesh,
        in_specs=placed,
        out_specs=(P("rep", "row", "col"), P("rep", "row")),
        check_vma=False,
    )
```

time: 57.4 us -> 43 us (0.75)
  Pallas kernels: 53.1 us -> 42.3 us
  local copies, waits for them, and re-layouts: 3.32 us -> 0 us
    pallas_call x1, Pallas kernels: 46.4 us -> 35.5 us  [per_device(): pl.pallas_call(functools.partial(merge_kernel, dims), out_shape=(resident...]
    unnamed x8 -> x0, local copies, waits for them, and re-layouts: 3.32 us -> none
where the time goes in v2:
time: 43 us; the launch traced here: 42.9 us
  Pallas kernels  42.3 us (98%)
  between operations  0.64 us (1%)
    pallas_call x1, Pallas kernels, per_device(): pl.pallas_call(functools.partial(merge_kernel, dims), out_shape=(resident...  35.5 us
    pallas_call x1, Pallas kernels, per_device(): pl.pallas_call(functools.partial(scale_kernel, dims, slots), out_shape=(j...  6.76 us

profile of v2, /device:TPU:0, one launch (start us, length us, event | category | flops | bytes accessed | tf_op | source)
XLA Modules:
  0.0 42.9 jit_solution(6569184178778407824)
XLA Ops:
  0.6 35.5 %merge.1 = (bf16[2,4096,1024]{2,1,0:T(8,128)(2,1)S(1)}, f32[8,2,8,128]{3,2,1,0:T(8,128)S(1)}) custom-call(bf16[2,4096,1024]{2,1,0:T(8,128)(2,1)} %codes.1, f32[2,4096]{1,0:T(2,128)} %prev_hbm.1, bf16[2,64,512]{2,1,0:T(8,128)(2,1)} %bitcast.1, bf16[2,64,512]{2,1,0:T(8,128)(2,1)} %b_hbm.1, f32[2,4096]{1,0:T(2,128)} %mag_hbm.1), custom_call_target="tpu_custom_call" | custom-call | tf_op jit(solution)/shard_map/merge/pallas_call | solution.py:309
  36.1 6.8 %rescale.1 = (bf16[2,4096,1024]{2,1,0:T(8,128)(2,1)}, f32[2,4096]{1,0:T(2,128)}) custom-call(bf16[2,4096,1024]{2,1,0:T(8,128)(2,1)S(1)} %get-tuple-element.4.merged, f32[8,2,8,128]{3,2,1,0:T(8,128)S(1)} %get-tuple-element.5.res), custom_call_target="tpu_custom_call" | custom-call | tf_op jit(solution)/shard_map/rescale/pallas_call | solution.py:345
